TPU v7x, 256 devices: a whole 4x4x8 slice. The times are simulated.
256 devices in a mesh: seq: 64 (over x, y_lo, z), rep: 4 (over y_hi, core).
Axes of the slice: x: 4, y: 4 (y_hi: 2, y_lo: 2; y = y_hi * 2 + y_lo), z: 8, core: 2. Of those that a mesh axis runs over, the one named last changes fastest.
Arguments:
- queries: bfloat16 [4, 16384, 384], P('rep', 'seq'), may hold values from -3 to 3
- keys: bfloat16 [4, 16384, 384], P('rep', 'seq'), may hold values from -9 to 9
- values: bfloat16 [4, 16384, 384], P('rep', 'seq'), may hold values from -6 to 6
- outputs: bfloat16 [4, 16384, 384], P('rep', 'seq'), may hold values from -6 to 6
- out_grad: bfloat16 [4, 16384, 768], P('rep', 'seq'), may hold values from -6 to 6
- out_weight: bfloat16 [384, 768], replicated, may hold values from -0.21875 to 0.21875
- slide_table: int32 [4, 128], P('rep'), may hold values from 0 to 63, never falling along the last dimension, each value on 1 to 4 neighbouring positions
Outputs:
- query_grad: bfloat16 [4, 16384, 384], P('rep', 'seq')
- key_grad: bfloat16 [4, 16384, 384], P('rep', 'seq')
- value_grad: bfloat16 [4, 16384, 384], P('rep', 'seq')
- weight_grad: float32 [384, 768], replicated
Inputs may be any that keep to these rules, and one draw needn't show every extreme that they name: `slide_table`: in each replica the slide numbers never fall along the units, every slide of 0 to 63 holds 1 to 4 units, and some slide holds exactly 4 units.
All inputs are finite; a program needn't handle non-finite values.
Results may differ from a plain program's by a relative error of at most 0.012.
Values may be sent and summed in bfloat16 or wider, within the bound.
A program may use at most 64 MiB of HBM per device.

v0:
```python
import math

import jax
import jax.numpy as jnp
from jax import lax
from jax.sharding import PartitionSpec as P

HEAD = 64
BLOCK = 128
SPAN_DEV = 2


def from_behind(value, axis, steps):
    count = lax.axis_size(axis)
    first, last = (max(0, -steps), min(count, count - steps))
    return lax.ppermute(value, axis, [(source, source + steps) for source in range(first, last)])


def slide_ids(table_row, device, row_count, count_dev):
    spots = device * row_count + jnp.arange(row_count, dtype=jnp.int32)
    units = spots // BLOCK
    which = units[:, None] == jnp.arange(table_row.shape[0], dtype=jnp.int32)[None, :]
    found = jnp.sum(jnp.where(which, table_row[None, :], 0), axis=1)
    inside = (device >= 0) & (device < count_dev)
    return jnp.where(inside, found, -1)


def shards(queries, keys, values, outputs, out_grad, out_weight, slide_table):
    att_scale = 1.0 / math.sqrt(HEAD)
    q_rows = queries[0]
    k_rows = keys[0]
    v_rows = values[0]
    o_rows = outputs[0]
    dy_rows = out_grad[0]
    table_row = slide_table[0]
    row_count, feat_count = q_rows.shape
    head_count = feat_count // HEAD
    count_dev = lax.axis_size("seq")
    device = lax.axis_index("seq")
    reach = min(SPAN_DEV, count_dev // 4)
    attn_grad = lax.dot_general(
        dy_rows, out_weight, (((1,), (1,)), ((), ())), preferred_element_type=jnp.float32
    ).astype(jnp.bfloat16)
    local_term = lax.dot_general(
        o_rows, dy_rows, (((0,), (0,)), ((), ())), preferred_element_type=jnp.float32
    )
    tile_count = lax.axis_size("rep") * count_dev * row_count
    weight_grad = lax.psum(local_term, ("seq", "rep")) / math.sqrt(tile_count)
    deltas = jnp.sum(
        (attn_grad.astype(jnp.float32) * o_rows.astype(jnp.float32)).reshape(
            row_count, head_count, HEAD
        ),
        axis=2,
    ).T
    own_ids = slide_ids(table_row, device, row_count, count_dev)
    q_heads = q_rows.reshape(row_count, head_count, HEAD)
    k_heads = k_rows.reshape(row_count, head_count, HEAD)
    v_heads = v_rows.reshape(row_count, head_count, HEAD)
    d_heads = attn_grad.reshape(row_count, head_count, HEAD)

    def first_visit(state, kv_block, other_ids):
        in_mask = own_ids[:, None] == other_ids[None, :]
        sums, numer = state
        key_block = kv_block[0].reshape(row_count, head_count, HEAD)
        value_block = kv_block[1].reshape(row_count, head_count, HEAD)
        scores = (
            jnp.einsum("qhd,khd->hqk", q_heads, key_block, preferred_element_type=jnp.float32)
            * att_scale
        )
        expo = jnp.where(in_mask[None], jnp.exp(scores), 0.0)
        d_prob = jnp.einsum(
            "qhd,khd->hqk", d_heads, value_block, preferred_element_type=jnp.float32
        )
        weighted = (expo * (d_prob - deltas[:, :, None])).astype(jnp.bfloat16)
        numer = numer + jnp.einsum(
            "hqk,khd->qhd", weighted, key_block, preferred_element_type=jnp.float32
        )
        return (sums + jnp.sum(expo, axis=2), numer)

    def second_visit(state, side_block, stat_block, other_ids):
        in_mask = other_ids[:, None] == own_ids[None, :]
        key_sum, value_sum = state
        q_visit = side_block[0].reshape(row_count, head_count, HEAD)
        d_visit = side_block[1].reshape(row_count, head_count, HEAD)
        scores = (
            jnp.einsum("qhd,khd->hqk", q_visit, k_heads, preferred_element_type=jnp.float32)
            * att_scale
        )
        expo = jnp.where(in_mask[None], jnp.exp(scores), 0.0)
        totals_in = jnp.where((other_ids >= 0)[None, :], stat_block[0], 1.0)
        probs = expo / totals_in[:, :, None]
        d_prob = jnp.einsum("qhd,khd->hqk", d_visit, v_heads, preferred_element_type=jnp.float32)
        d_score = (probs * (d_prob - stat_block[1][:, :, None])).astype(jnp.bfloat16)
        value_sum = value_sum + jnp.einsum(
            "hqk,qhd->khd", probs.astype(jnp.bfloat16), d_visit, preferred_element_type=jnp.float32
        )
        key_sum = key_sum + jnp.einsum(
            "hqk,qhd->khd", d_score, q_visit, preferred_element_type=jnp.float32
        )
        return (key_sum, value_sum)

    kv_own = jnp.stack([k_rows, v_rows])
    first_state = (
        jnp.zeros((head_count, row_count), jnp.float32),
        jnp.zeros((row_count, head_count, HEAD), jnp.float32),
    )
    first_state = first_visit(first_state, kv_own, own_ids)
    for distance in range(1, reach + 1):
        for direction in range(2):
            offset = distance if direction == 0 else -distance
            kv_in = from_behind(kv_own, "seq", offset)
            first_state = first_visit(
                first_state, kv_in, slide_ids(table_row, device - offset, row_count, count_dev)
            )
    totals, numer = first_state
    query_grad = (
        (att_scale * numer / totals.T[:, :, None])
        .astype(jnp.bfloat16)
        .reshape(row_count, feat_count)
    )
    side_own = jnp.stack([q_rows, attn_grad])
    stat_own = jnp.stack([totals, deltas])
    zero_heads = jnp.zeros((row_count, head_count, HEAD), jnp.float32)
    second_state = second_visit((zero_heads, zero_heads), side_own, stat_own, own_ids)
    for distance in range(1, reach + 1):
        for direction in range(2):
            offset = distance if direction == 0 else -distance
            side_in = from_behind(side_own, "seq", offset)
            stat_in = from_behind(stat_own, "seq", offset)
            second_state = second_visit(
                second_state,
                side_in,
                stat_in,
                slide_ids(table_row, device - offset, row_count, count_dev),
            )
    key_sum, value_sum = second_state
    key_grad = (att_scale * key_sum).astype(jnp.bfloat16).reshape(row_count, feat_count)
    value_grad = value_sum.astype(jnp.bfloat16).reshape(row_count, feat_count)
    return (query_grad[None], key_grad[None], value_grad[None], weight_grad)


def solution(mesh):
    return jax.shard_map(
        shards,
        mesh=mesh,
        in_specs=(
            P("rep", "seq", None),
            P("rep", "seq", None),
            P("rep", "seq", None),
            P("rep", "seq", None),
            P("rep", "seq", None),
            P(),
            P("rep", None),
        ),
        out_specs=(P("rep", "seq", None), P("rep", "seq", None), P("rep", "seq", None), P()),
        check_vma=False,
    )
```

profile of v0, /device:TPU:25, one launch (start us, length us, event | category | flops | bytes accessed | tf_op | source)
XLA Modules:
  0.0 308.7 jit_solution(14594314940746458659)
XLA Ops:
  10.3 8.1 %collective-permute-start.3 = (bf16[2,256,384]{1,2,0:T(8,128)(2,1)}, bf16[2,256,384]{1,2,0:T(8,128)(2,1)}, u32[]{:S(2)}, u32[]{:S(2)}) collective-permute-start(bf16[2,256,384]{1,2,0:T(8,128)(2,1)} %pad_maximum_fusion), channel_id=1, source_target_pairs={{8,0},{12,4},{16,8},{20,12},{24,16},{28,20},{32,24},{36,28},{40,32... | collective-permute-start | bytes 1179656 | tf_op jit(solution)/shard_map/ppermute | solution.py:16
  20.3 2.6 collective-permute-start
  23.0 5.2 %collective-permute-start.1 = (bf16[2,256,384]{1,2,0:T(8,128)(2,1)}, bf16[2,256,384]{1,2,0:T(8,128)(2,1)}, u32[]{:S(2)}, u32[]{:S(2)}) collective-permute-start(bf16[2,256,384]{1,2,0:T(8,128)(2,1)} %pad_maximum_fusion), channel_id=1, source_target_pairs={{4,0},{8,4},{12,8},{16,12},{20,16},{24,20},{28,24},{32,28},{36,32}... | collective-permute-start | bytes 1179656 | tf_op jit(solution)/shard_map/ppermute | solution.py:16
  36.7 2.3 fusion.85
  41.9 2.4 convolution_bitcast_fusion
  44.4 5.5 %collective-permute-start.6 = (bf16[2,256,384]{2,1,0:T(8,128)(2,1)}, bf16[2,256,384]{2,1,0:T(8,128)(2,1)}, u32[]{:S(2)}, u32[]{:S(2)}) collective-permute-start(bf16[2,256,384]{2,1,0:T(8,128)(2,1)} %pad_maximum_fusion.1), channel_id=1, source_target_pairs={{4,0},{8,4},{12,8},{16,12},{20,16},{24,20},{28,24},{32,28},{36,32}... | collective-permute-start | bytes 1179656 | tf_op jit(solution)/shard_map/ppermute | solution.py:16
  56.2 2.3 fusion.83
  59.3 6.4 %collective-permute-start.10 = (bf16[2,256,384]{2,1,0:T(8,128)(2,1)}, bf16[2,256,384]{2,1,0:T(8,128)(2,1)}, u32[]{:S(2)}, u32[]{:S(2)}) collective-permute-start(bf16[2,256,384]{2,1,0:T(8,128)(2,1)} %pad_maximum_fusion.1), channel_id=1, source_target_pairs={{8,0},{12,4},{16,8},{20,12},{24,16},{28,20},{32,24},{36,28},{40,32... | collective-permute-start | bytes 1179656 | tf_op jit(solution)/shard_map/ppermute | solution.py:16
  67.4 1.9 copy.147
  69.4 2.6 fusion.86
  78.9 5.5 %collective-permute-start.7 = (f32[2,6,256]{2,1,0:T(8,128)}, f32[2,6,256]{2,1,0:T(8,128)}, u32[]{:S(2)}, u32[]{:S(2)}) collective-permute-start(f32[2,6,256]{2,1,0:T(8,128)} %pad_maximum_fusion.2), channel_id=1, source_target_pairs={{4,0},{8,4},{12,8},{16,12},{20,16},{24,20},{28,24},{32,28},{36,32}... | collective-permute-start | bytes 36872 | tf_op jit(solution)/shard_map/ppermute | solution.py:16
  92.4 2.5 fusion.88
  96.4 6.6 %collective-permute-start.11 = (f32[2,6,256]{2,1,0:T(8,128)}, f32[2,6,256]{2,1,0:T(8,128)}, u32[]{:S(2)}, u32[]{:S(2)}) collective-permute-start(f32[2,6,256]{2,1,0:T(8,128)} %pad_maximum_fusion.2), channel_id=1, source_target_pairs={{8,0},{12,4},{16,8},{20,12},{24,16},{28,20},{32,24},{36,28},{40,32... | collective-permute-start | bytes 36872 | tf_op jit(solution)/shard_map/ppermute | solution.py:16
  104.9 2.6 fusion.41
  112.9 2.8 fusion.17
  115.7 3.1 %fusion.21 = f32[256,6,64]{0,2,1:T(8,128)} fusion(f32[256,6,64]{0,2,1:T(8,128)} %convolution_bitcast_fusion, bf16[256,6,64]{0,2,1:T(8,128)(2,1)} %bitcast.201, f32[6,256,256]{2,1,0:T(8,128)} %get-tuple-element.73, bf16[256,6,64]{0,2,1:T(8,128)(2,1)S(1)} %bitcast.184, bf16[256,6,64]{0,2,1:T(8,128)(2,1)} %bitcast.199, f32[6,256]{1,0:T(8,128)S(1)} %bitcast.224), kind=kOutput, calls=%fused_computation.42 | convolution fusion | flops 101941248 | bytes 2955264 | tf_op jit(solution)/shard_map/hqk,khd->qhd/dot_general | solution.py:75
  120.7 2.6 fusion.90
  127.0 2.7 fusion.15
  131.1 3.1 fusion.13
  134.9 2.7 fusion.35
  139.1 3.1 fusion.11
  143.4 2.4 fusion.31
  151.1 148.4 %all-reduce.2.cloned.1.call-done = f32[384,768]{1,0:T(8,128)} async-done(((f32[384,768]{1,0:T(8,128)}), f32[384,768]{1,0:T(8,128)}) %all-reduce.2.cloned.1.call-update) | async-done | bytes 1179664 | tf_op jit(solution)/shard_map/psum | solution.py:48
  299.5 2.4 broadcast_multiply_fusion
  (185 shorter events, 64.1 us)
Async XLA Ops:
  7.2 21.0 %copy-start = (bf16[384,768]{1,0:T(8,128)(2,1)S(1)}, bf16[384,768]{1,0:T(8,128)(2,1)}, u32[]{:S(2)}) copy-start(bf16[384,768]{1,0:T(8,128)(2,1)} %param.12) | copy-start | bytes 1769476
  7.2 21.0 %copy-start.9 = (bf16[1,256,384]{2,1,0:T(8,128)(2,1)S(1)}, bf16[1,256,384]{2,1,0:T(8,128)(2,1)}, u32[]{:S(2)}) copy-start(bf16[1,256,384]{2,1,0:T(8,128)(2,1)} %param.10) | copy-start | bytes 589828
  7.2 21.0 %copy-start.5 = (bf16[1,256,768]{2,1,0:T(8,128)(2,1)S(1)}, bf16[1,256,768]{2,1,0:T(8,128)(2,1)}, u32[]{:S(2)}) copy-start(bf16[1,256,768]{2,1,0:T(8,128)(2,1)} %param.11) | copy-start | bytes 1179652
  7.2 292.3 %all-reduce.2.cloned.1.call-start = ((), (), s32[]{:S(2)}) async-start(), calls=%async_computation | async-start | bytes 2359296 | tf_op jit(solution)/shard_map/psum | solution.py:48
  8.4 20.2 %copy-start.15 = (bf16[1,256,384]{2,1,0:T(8,128)(2,1)S(1)}, bf16[1,256,384]{2,1,0:T(8,128)(2,1)}, u32[]{:S(2)}) copy-start(bf16[1,256,384]{2,1,0:T(8,128)(2,1)} %param.7) | copy-start | bytes 589828
  10.3 34.1 %collective-permute-start.3 = (bf16[2,256,384]{1,2,0:T(8,128)(2,1)}, bf16[2,256,384]{1,2,0:T(8,128)(2,1)}, u32[]{:S(2)}, u32[]{:S(2)}) collective-permute-start(bf16[2,256,384]{1,2,0:T(8,128)(2,1)} %pad_maximum_fusion), channel_id=1, source_target_pairs={{8,0},{12,4},{16,8},{20,12},{24,16},{28,20},{32,24},{36,28},{40,32... | collective-permute-start | bytes 1179656 | tf_op jit(solution)/shard_map/ppermute | solution.py:16
  18.4 34.8 %collective-permute-start.2 = (bf16[2,256,384]{1,2,0:T(8,128)(2,1)}, bf16[2,256,384]{1,2,0:T(8,128)(2,1)}, u32[]{:S(2)}, u32[]{:S(2)}) collective-permute-start(bf16[2,256,384]{1,2,0:T(8,128)(2,1)} %pad_maximum_fusion), channel_id=1, source_target_pairs={{0,8},{4,12},{8,16},{12,20},{16,24},{20,28},{24,32},{28,36},{32,40... | collective-permute-start | bytes 1179656 | tf_op jit(solution)/shard_map/ppermute | solution.py:16
  20.3 38.2 %collective-permute-start = (bf16[2,256,384]{1,2,0:T(8,128)(2,1)}, bf16[2,256,384]{1,2,0:T(8,128)(2,1)S(1)}, u32[]{:S(2)}, u32[]{:S(2)}) collective-permute-start(bf16[2,256,384]{1,2,0:T(8,128)(2,1)} %pad_maximum_fusion), channel_id=1, source_target_pairs={{0,4},{4,8},{8,12},{12,16},{16,20},{20,24},{24,28},{28,32},{32,36}... | collective-permute-start | bytes 1179656 | tf_op jit(solution)/shard_map/ppermute | solution.py:16
  23.0 49.0 %collective-permute-start.1 = (bf16[2,256,384]{1,2,0:T(8,128)(2,1)}, bf16[2,256,384]{1,2,0:T(8,128)(2,1)}, u32[]{:S(2)}, u32[]{:S(2)}) collective-permute-start(bf16[2,256,384]{1,2,0:T(8,128)(2,1)} %pad_maximum_fusion), channel_id=1, source_target_pairs={{4,0},{8,4},{12,8},{16,12},{20,16},{24,20},{28,24},{32,28},{36,32}... | collective-permute-start | bytes 1179656 | tf_op jit(solution)/shard_map/ppermute | solution.py:16
  29.4 49.5 %collective-permute-start.4 = (bf16[2,256,384]{2,1,0:T(8,128)(2,1)}, bf16[2,256,384]{2,1,0:T(8,128)(2,1)}, u32[]{:S(2)}, u32[]{:S(2)}) collective-permute-start(bf16[2,256,384]{2,1,0:T(8,128)(2,1)} %pad_maximum_fusion.1), channel_id=1, source_target_pairs={{0,4},{4,8},{8,12},{12,16},{16,20},{20,24},{24,28},{28,32},{32,36}... | collective-permute-start | bytes 1179656 | tf_op jit(solution)/shard_map/ppermute | solution.py:16
  33.1 40.7 %copy-start.20 = (bf16[1,256,384]{1,2,0:T(8,128)(2,1)}, bf16[1,256,384]{1,2,0:T(8,128)(2,1)S(1)}, u32[]{:S(2)}) copy-start(bf16[1,256,384]{1,2,0:T(8,128)(2,1)S(1)} %copy.125) | copy-start | bytes 589828
  39.5 4.9 %copy-start.1 = (f32[6,256,256]{1,2,0:T(8,128)}, f32[6,256,256]{1,2,0:T(8,128)S(1)}, u32[]{:S(2)}) copy-start(f32[6,256,256]{1,2,0:T(8,128)S(1)} %convolution_subtract_fusion) | copy-start | bytes 4718596
  44.4 43.5 %collective-permute-start.6 = (bf16[2,256,384]{2,1,0:T(8,128)(2,1)}, bf16[2,256,384]{2,1,0:T(8,128)(2,1)}, u32[]{:S(2)}, u32[]{:S(2)}) collective-permute-start(bf16[2,256,384]{2,1,0:T(8,128)(2,1)} %pad_maximum_fusion.1), channel_id=1, source_target_pairs={{4,0},{8,4},{12,8},{16,12},{20,16},{24,20},{28,24},{32,28},{36,32}... | collective-permute-start | bytes 1179656 | tf_op jit(solution)/shard_map/ppermute | solution.py:16
  53.2 43.2 %collective-permute-start.8 = (bf16[2,256,384]{2,1,0:T(8,128)(2,1)}, bf16[2,256,384]{2,1,0:T(8,128)(2,1)}, u32[]{:S(2)}, u32[]{:S(2)}) collective-permute-start(bf16[2,256,384]{2,1,0:T(8,128)(2,1)} %pad_maximum_fusion.1), channel_id=1, source_target_pairs={{0,8},{4,12},{8,16},{12,20},{16,24},{20,28},{24,32},{28,36},{32,40... | collective-permute-start | bytes 1179656 | tf_op jit(solution)/shard_map/ppermute | solution.py:16
  56.2 9.5 %copy-start.10 = (bf16[1,256,384]{1,2,0:T(8,128)(2,1)}, bf16[1,256,384]{1,2,0:T(8,128)(2,1)S(1)}, u32[]{:S(2)}) copy-start(bf16[1,256,384]{1,2,0:T(8,128)(2,1)S(1)} %get-tuple-element.46) | copy-start | bytes 589828
  59.3 51.1 %collective-permute-start.10 = (bf16[2,256,384]{2,1,0:T(8,128)(2,1)}, bf16[2,256,384]{2,1,0:T(8,128)(2,1)}, u32[]{:S(2)}, u32[]{:S(2)}) collective-permute-start(bf16[2,256,384]{2,1,0:T(8,128)(2,1)} %pad_maximum_fusion.1), channel_id=1, source_target_pairs={{8,0},{12,4},{16,8},{20,12},{24,16},{28,20},{32,24},{36,28},{40,32... | collective-permute-start | bytes 1179656 | tf_op jit(solution)/shard_map/ppermute | solution.py:16
  77.0 48.5 %collective-permute-start.5 = (f32[2,6,256]{2,1,0:T(8,128)}, f32[2,6,256]{2,1,0:T(8,128)}, u32[]{:S(2)}, u32[]{:S(2)}) collective-permute-start(f32[2,6,256]{2,1,0:T(8,128)} %pad_maximum_fusion.2), channel_id=1, source_target_pairs={{0,4},{4,8},{8,12},{12,16},{16,20},{20,24},{24,28},{28,32},{32,36}... | collective-permute-start | bytes 36872 | tf_op jit(solution)/shard_map/ppermute | solution.py:16
  78.9 50.8 %collective-permute-start.7 = (f32[2,6,256]{2,1,0:T(8,128)}, f32[2,6,256]{2,1,0:T(8,128)}, u32[]{:S(2)}, u32[]{:S(2)}) collective-permute-start(f32[2,6,256]{2,1,0:T(8,128)} %pad_maximum_fusion.2), channel_id=1, source_target_pairs={{4,0},{8,4},{12,8},{16,12},{20,16},{24,20},{28,24},{32,28},{36,32}... | collective-permute-start | bytes 36872 | tf_op jit(solution)/shard_map/ppermute | solution.py:16
  86.3 6.1 %copy-start.22 = (bf16[1,256,384]{1,2,0:T(8,128)(2,1)}, bf16[1,256,384]{1,2,0:T(8,128)(2,1)S(1)}, u32[]{:S(2)}) copy-start(bf16[1,256,384]{1,2,0:T(8,128)(2,1)S(1)} %copy.151) | copy-start | bytes 589828
  87.9 49.8 %collective-permute-start.9 = (f32[2,6,256]{2,1,0:T(8,128)}, f32[2,6,256]{2,1,0:T(8,128)}, u32[]{:S(2)}, u32[]{:S(2)}) collective-permute-start(f32[2,6,256]{2,1,0:T(8,128)} %pad_maximum_fusion.2), channel_id=1, source_target_pairs={{0,8},{4,12},{8,16},{12,20},{16,24},{20,28},{24,32},{28,36},{32,40... | collective-permute-start | bytes 36872 | tf_op jit(solution)/shard_map/ppermute | solution.py:16
  96.4 37.8 %collective-permute-start.11 = (f32[2,6,256]{2,1,0:T(8,128)}, f32[2,6,256]{2,1,0:T(8,128)}, u32[]{:S(2)}, u32[]{:S(2)}) collective-permute-start(f32[2,6,256]{2,1,0:T(8,128)} %pad_maximum_fusion.2), channel_id=1, source_target_pairs={{8,0},{12,4},{16,8},{20,12},{24,16},{28,20},{32,24},{36,28},{40,32... | collective-permute-start | bytes 36872 | tf_op jit(solution)/shard_map/ppermute | solution.py:16
  120.7 4.6 %copy-start.19 = (bf16[1,256,384]{2,1,0:T(8,128)(2,1)S(1)}, bf16[1,256,384]{2,1,0:T(8,128)(2,1)}, u32[]{:S(2)}) copy-start(bf16[1,256,384]{2,1,0:T(8,128)(2,1)} %get-tuple-element.33) | copy-start | bytes 589828
  120.7 5.5 %copy-start.48 = (pred[256]{0:T(512)(128)(4,1)S(1)}, pred[256]{0:T(512)(128)(4,1)}, u32[]{:S(2)}) copy-start(pred[256]{0:T(512)(128)(4,1)} %get-tuple-element.76) | copy-start | bytes 772
  120.7 6.2 %copy-start.6 = (f32[6,256,256]{1,2,0:T(8,128)S(1)}, f32[6,256,256]{1,2,0:T(8,128)}, u32[]{:S(2)}) copy-start(f32[6,256,256]{1,2,0:T(8,128)} %fusion.87) | copy-start | bytes 4718596
  (40 other events, 114.6 us)
Sparse Core Ops, SparseCore 0:
  32.9 266.6 all-reduce.1
where the time goes:
time: 313 us; the launch traced here: 309 us
  waiting for transfers between devices  148 us (47%)
  matrix products  53.2 us (17%)
  starting transfers between devices  49.4 us (16%)
  local copies, waits for them, and re-layouts  31.3 us (10%)
  between operations  14.8 us (5%)
  other arithmetic  11.5 us (4%)
    psum x1, waiting for transfers between devices, shards(): weight_grad = lax.psum(local_term, ('seq', 'rep')) / math.sqrt(tile_count)  148 us
    ppermute x12, starting transfers between devices, from_behind(): lax.ppermute(value, axis, [(source, source + steps) for source in range(f...  49.4 us
    dot_general x5, matrix products, second_visit(): jnp.einsum('hqk,qhd->khd', d_score, q_visit, preferred_element_type=jnp.f...  12.4 us
    dot_general x5, matrix products, first_visit(): jnp.einsum('hqk,khd->qhd', weighted, key_block, preferred_element_type=jn...  11.7 us
    dot_general x5, matrix products, first_visit(): jnp.einsum('qhd,khd->hqk', q_heads, key_block, preferred_element_type=jnp...  10.6 us
    dot_general x4, matrix products, second_visit(): jnp.einsum('qhd,khd->hqk', q_visit, k_heads, preferred_element_type=jnp.f...  8.33 us
    slice x8, local copies, waits for them, and re-layouts, second_visit(): d_visit = side_block[1].reshape(row_count, head_count, HEAD)  8.23 us
    dot_general x5, matrix products, second_visit(): jnp.einsum('hqk,qhd->khd', probs.astype(jnp.bfloat16), d_visit, preferred...  7.98 us
  transfers between devices with their start and end apart: 13, of which 1 were waited for; matrix products, arithmetic and copies ran while one was open for 29% of the time, Pallas kernels for 0%

commit v1 on v0

v1 whole, which is shorter than its diff:
```python
import functools
import math

import jax
import jax.numpy as jnp
from jax import lax
from jax.experimental import pallas as pl
from jax.experimental.pallas import tpu as pltpu
from jax.sharding import PartitionSpec as P

HEAD = 64
UNIT = 128
PAIR = 128
ROWS = 256
FEATS = 384
WIDTH = 768
PAIRS = FEATS // PAIR
HALF = FEATS // 2
TILE = 16
TILES = HALF * WIDTH // (TILE * 128)
GRID = (4, 2, 8, 2, 2)
FAR = -1e30
MESH = pl.DeviceIdType.MESH
F32 = jnp.float32
BF16 = jnp.bfloat16


def nt(a, b):
    return lax.dot_general(a, b, (((1,), (1,)), ((), ())), preferred_element_type=F32)


def nn(a, b):
    return lax.dot_general(a, b, (((1,), (0,)), ((), ())), preferred_element_type=F32)


def roll_half(x):
    return jnp.concatenate([x[:, HEAD:], x[:, :HEAD]], axis=1)


def lanes(shape):
    return lax.broadcasted_iota(jnp.int32, shape, 1)


def below(limit, x, y):
    return jnp.where(lanes(x.shape) < limit, x, y)


def kernel(
    grid, tab, q, k, v, o, dy, w,
    dq, dk, dv, wg,
    d_own, snd_l, snd_r, rcv_l, rcv_r, del_own, del_sl, del_sr, del_rl, del_rr,
    ret_sl, ret_sr, ret_rl, ret_rr, bias, win, p_buf, s_buf, q_turn,
    term, core_in, plane_out, plane_in, line, final,
    halo_send, halo_recv, del_send, del_recv, ret_send, ret_recv,
    core_send, core_recv, plane_send, plane_recv, line_send, line_recv,
    share_send, share_recv, swap_send, swap_recv,
):
    nx, nyl, nz, nyh, ncore = grid
    ny = nyl * nyh
    nplane = nx * ny
    depth = -(-TILES // nplane) * TILE
    nseq = nx * nyl * nz
    seq = lax.axis_index("seq")
    rep = lax.axis_index("rep")
    z = lax.rem(seq, nz)
    yl = lax.rem(seq // nz, nyl)
    x = seq // (nz * nyl)
    core = lax.rem(rep, ncore)
    yh = rep // ncore
    spot = x * ny + yh * nyl + yl
    left = lax.rem(seq + nseq - 1, nseq)
    right = lax.rem(seq + 1, nseq)
    to_left = (left, rep)
    to_right = (right, rep)
    to_core = (seq, yh * ncore + (ncore - 1 - core))

    def plane_peer(offset):
        other = lax.rem(spot + offset, nplane)
        oy = lax.rem(other, ny)
        device = ((other // ny) * nyl + lax.rem(oy, nyl)) * nz + z, (oy // nyl) * ncore + core
        return other, device

    def line_peer(offset):
        return ((seq - z) + lax.rem(z + offset, nz), rep)

    barrier = pltpu.get_barrier_semaphore()
    for peer in (to_left, to_right, to_core):
        pl.semaphore_signal(barrier, inc=1, device_id=peer, device_id_type=MESH)
    for offset in range(1, nplane):
        pl.semaphore_signal(barrier, inc=1, device_id=plane_peer(offset)[1], device_id_type=MESH)
    for offset in range(1, nz):
        pl.semaphore_signal(barrier, inc=1, device_id=line_peer(offset), device_id_type=MESH)

    first = 2 * seq
    last_unit = 2 * nseq - 1

    def unit(step):
        return tab[0, jnp.clip(first + step, 0, last_unit)]

    flag = lambda cond: jnp.where(cond, 1, 0)
    l2, l1, a, b, r1, r2 = (unit(step) for step in (-2, -1, 0, 1, 2, 3))
    ab = flag(a == b)
    l21 = flag(l2 == l1)
    r12 = flag(r1 == r2)
    cross_l = flag(l1 == a) * flag(seq > 0)
    cross_r = flag(b == r1) * flag(seq < nseq - 1)
    split_r = cross_l * ab * l21
    split_l = cross_r * ab * r12
    recv_l = cross_l * ab * (1 - l21)
    sent_l = cross_l * (1 - ab)
    sent_r = cross_r * (1 - ab) * r12
    recv_r = cross_r * (1 - r12)

    low = lambda cond: HEAD * cond
    high = lambda cond: 2 * HEAD - HEAD * cond
    pick = lambda cond, yes, no: jnp.where(cond > 0, yes, no)

    def low_from(cond, x, y):
        return below(low(cond), roll_half(y), x)

    def high_from(cond, x, y):
        return below(high(cond), x, roll_half(y))

    def copy(src, dst, send, recv, peer):
        return pltpu.make_async_remote_copy(
            src_ref=src, dst_ref=dst, send_sem=send, recv_sem=recv,
            device_id=peer, device_id_type=MESH,
        )

    d_own[...] = nt(dy[0], w[...]).astype(BF16)
    prod = d_own[...].astype(F32) * o[0].astype(F32)
    upper = prod.astype(BF16)
    lower = (prod - upper.astype(F32)).astype(BF16)
    chooser = (
        lax.broadcasted_iota(jnp.int32, (8, FEATS), 1) // HEAD
        == lax.broadcasted_iota(jnp.int32, (8, FEATS), 0)
    ).astype(F32).astype(BF16)
    del_own[...] = nt(chooser, upper) + nt(chooser, lower)

    for h in range(2 * PAIRS):
        even = h - h % 2
        da, db = del_own[h:h + 1, :UNIT], del_own[h:h + 1, UNIT:]
        if h % 2:
            db_even = del_own[even:even + 1, UNIT:]
            del_sl[h:h + 1] = below(UNIT * split_r, db_even, da)
            del_sr[h:h + 1] = db
        else:
            da_odd = del_own[h + 1:h + 2, :UNIT]
            del_sl[h:h + 1] = da
            del_sr[h:h + 1] = below(UNIT * split_l, da_odd, db)
    del_sl[6:8] = jnp.zeros((2, UNIT), F32)
    del_sr[6:8] = jnp.zeros((2, UNIT), F32)

    sources = (q, k, v, None)
    for p in range(PAIRS):
        cols = slice(p * PAIR, (p + 1) * PAIR)
        for i, src in enumerate(sources):
            if src is None:
                ua, ub = d_own[:UNIT, cols], d_own[UNIT:, cols]
            else:
                ua, ub = src[0, :UNIT, cols], src[0, UNIT:, cols]
            snd_l[p, i] = high_from(split_r, ua, ub)
            snd_r[p, i] = low_from(split_l, ub, ua)

    for j in range(WIDTH // 128):
        block = lax.dot_general(
            o[0], dy[0, :, j * 128:(j + 1) * 128],
            (((0,), (0,)), ((), ())), preferred_element_type=F32,
        ).astype(BF16)
        for h in range(2):
            term[h, j * HALF:(j + 1) * HALF] = block[h * HALF:(h + 1) * HALF]

    pl.semaphore_wait(barrier, 3 + (nplane - 1) + (nz - 1))

    sends = []

    def go(c):
        c.start()
        sends.append(c)
        return c

    deltas_in = [
        go(copy(del_sl, del_rr, del_send.at[0], del_recv.at[0], to_left)),
        go(copy(del_sr, del_rl, del_send.at[1], del_recv.at[1], to_right)),
    ]
    halo_in = []
    for p in range(PAIRS):
        halo_in.append([
            go(copy(snd_l.at[p], rcv_r.at[p], halo_send.at[0, p], halo_recv.at[0, p], to_left)),
            go(copy(snd_r.at[p], rcv_l.at[p], halo_send.at[1, p], halo_recv.at[1, p], to_right)),
        ])
        if p == 0:
            core_copy = go(copy(term.at[1 - core], core_in, core_send, core_recv, to_core))

    for par in range(2):
        mine_away = split_l if par else split_r
        theirs = split_r if par else split_l
        kinds = (
            pick(recv_l + theirs, a, -3),
            pick(sent_l + mine_away, -1, a),
            pick(sent_r + mine_away, -2, b),
            pick(recv_r + theirs, b, -4),
        )
        for i in range(4):
            for j in range(4):
                level = jnp.where(kinds[i] == kinds[j], F32(-2.0), F32(FAR))
                bias[par, i * UNIT:(i + 1) * UNIT, j * UNIT:(j + 1) * UNIT] = jnp.full(
                    (UNIT, UNIT), level, F32
                )

    core_copy.wait_recv()
    plane_out[...] = (term[core].astype(F32) + core_in[...].astype(F32)).astype(BF16)

    def chunk(index):
        return pl.ds(pl.multiple_of((index * TILES) // nplane * TILE, TILE), depth)

    plane_copies = []
    for offset in range(1, nplane):
        other, peer = plane_peer(offset)
        plane_copies.append(go(copy(
            plane_out.at[chunk(other)], plane_in.at[offset - 1],
            plane_send.at[offset - 1], plane_recv.at[offset - 1], peer,
        )))

    scale = 0.125 * math.log2(math.e)

    def attend(p):
        for c in halo_in[p]:
            c.wait_recv()
        cols = slice(p * PAIR, (p + 1) * PAIR)
        for i, src in enumerate(sources):
            win[i, :UNIT] = low_from(split_l, rcv_l[p, i], rcv_r[p, i])
            win[i, UNIT:3 * UNIT] = d_own[:, cols] if src is None else src[0, :, cols]
            win[i, 3 * UNIT:] = high_from(split_r, rcv_r[p, i], rcv_l[p, i])
        key_turn = win[1].T
        d_keys, d_values = [], []
        for par in range(2):
            h = 2 * p + par
            own = del_own[h:h + 1]
            if par:
                d0 = del_rl[h:h + 1]
                d3 = below(UNIT * split_r, del_rl[h - 1:h], del_rr[h:h + 1])
                zero = jnp.zeros_like(win[1])
                key_one = below(HEAD, zero, win[1])
                value_one = below(HEAD, zero, win[2])
            else:
                d0 = below(UNIT * split_l, del_rr[h + 1:h + 2], del_rl[h:h + 1])
                d3 = del_rr[h:h + 1]
                zero = jnp.zeros_like(win[1])
                key_one = below(HEAD, win[1], zero)
                value_one = below(HEAD, win[2], zero)
            delta_halves = (
                jnp.concatenate([d0, own[:, :UNIT]], axis=1),
                jnp.concatenate([own[:, UNIT:], d3], axis=1),
            )
            for half in range(2):
                part = slice(half * 256, half * 256 + 256)
                scores = nt(key_one, win[0, part])
                expo = jnp.exp2(scores * scale + bias[par, :, part])
                totals = jnp.sum(expo, axis=0, keepdims=True)
                probs = expo * (1.0 / totals)
                d_prob = nt(value_one, win[3, part])
                d_score = (probs * (d_prob - delta_halves[half])).astype(BF16)
                p_buf[:, part] = probs.astype(BF16)
                s_buf[:, part] = d_score
                q_turn[par * HEAD:(par + 1) * HEAD, part] = nn(
                    key_turn[par * HEAD:(par + 1) * HEAD], d_score
                )
            d_values.append(nn(p_buf[...], win[3]))
            d_keys.append(nn(s_buf[...], win[0]))
        grads = (
            (dq, 0.125 * q_turn[...].T),
            (dk, 0.125 * below(HEAD, d_keys[0], d_keys[1])),
            (dv, below(HEAD, d_values[0], d_values[1])),
        )
        for i, (out, grad) in enumerate(grads):
            grad = grad.astype(BF16)
            out[0, :, cols] = grad[UNIT:3 * UNIT]
            before, after = grad[:UNIT], grad[3 * UNIT:]
            ret_sl[p, i] = low_from(split_r, before, after)
            ret_sr[p, i] = high_from(split_l, after, before)
        return [
            go(copy(ret_sl.at[p], ret_rr.at[p], ret_send.at[0, p], ret_recv.at[0, p], to_left)),
            go(copy(ret_sr.at[p], ret_rl.at[p], ret_send.at[1, p], ret_recv.at[1, p], to_right)),
        ]

    for c in deltas_in:
        c.wait_recv()
    returns = [attend(0)]

    for c in plane_copies:
        c.wait_recv()
    total = plane_out[chunk(spot)].astype(F32)
    for offset in range(1, nplane):
        total = total + plane_in[offset - 1].astype(F32)
    line[z] = total.astype(BF16)
    line_copies = []
    for offset in range(1, nz):
        line_copies.append(go(copy(
            line.at[z], line.at[z], line_send.at[offset - 1], line_recv.at[offset - 1],
            line_peer(offset),
        )))

    returns.append(attend(1))

    for c in line_copies:
        c.wait_recv()
    total = line[0].astype(F32)
    for index in range(1, nz):
        total = total + line[index].astype(F32)
    norm = 1.0 / math.sqrt(nseq * ROWS * nyh * ncore)
    final[core, spot] = (total * norm).astype(BF16)
    share_copies = []
    for offset in range(1, nplane):
        _, peer = plane_peer(offset)
        share_copies.append(go(copy(
            final.at[core, spot], final.at[core, spot],
            share_send.at[offset - 1], share_recv.at[offset - 1], peer,
        )))

    returns.append(attend(2))

    for c in share_copies:
        c.wait_recv()
    swap = go(copy(final.at[core], final.at[core], swap_send, swap_recv, to_core))

    for p in range(PAIRS):
        for c in returns[p]:
            c.wait_recv()
        cols = slice(p * PAIR, (p + 1) * PAIR)
        for i, out in enumerate((dq, dk, dv)):
            from_l, from_r = ret_rl[p, i], ret_rr[p, i]
            ua, ub = out[0, :UNIT, cols], out[0, UNIT:, cols]
            ua = high_from(split_l, ua, from_r)
            out[0, :UNIT, cols] = below(HEAD * (2 * sent_l + split_r), from_l, ua)
            ub = low_from(split_r, ub, from_l)
            out[0, UNIT:, cols] = below(
                2 * HEAD - HEAD * (2 * sent_r + split_l), ub, from_r
            )

    swap.wait_recv()
    for h in range(2):
        for index in range(nplane):
            begin = (index * TILES) // nplane
            end = ((index + 1) * TILES) // nplane
            for t in range(begin, end):
                j, row = divmod(t * TILE, HALF)
                wg[h * HALF + row:h * HALF + row + TILE, j * 128:(j + 1) * 128] = final[
                    h, index, (t - begin) * TILE:(t - begin + 1) * TILE
                ].astype(F32)

    for c in sends:
        c.wait_send()


def shards(grid, queries, keys, values, outputs, out_grad, out_weight, slide_table):
    nx, nyl, nz, nyh, ncore = grid
    nplane = nx * nyl * nyh
    depth = -(-TILES // nplane) * TILE
    dma = pltpu.SemaphoreType.DMA
    vmem = pl.BlockSpec(memory_space=pltpu.VMEM)
    part = (1, ROWS, FEATS)
    halo = (PAIRS, 4, UNIT, PAIR)
    back = (PAIRS, 3, UNIT, PAIR)
    return pl.pallas_call(
        functools.partial(kernel, grid),
        out_shape=[jax.ShapeDtypeStruct(part, BF16)] * 3
        + [jax.ShapeDtypeStruct((FEATS, WIDTH), F32)],
        in_specs=[pl.BlockSpec(memory_space=pltpu.SMEM)] + [vmem] * 6,
        out_specs=[vmem] * 4,
        scratch_shapes=[
            pltpu.VMEM((ROWS, FEATS), BF16),
            pltpu.VMEM(halo, BF16),
            pltpu.VMEM(halo, BF16),
            pltpu.VMEM(halo, BF16),
            pltpu.VMEM(halo, BF16),
            pltpu.VMEM((8, ROWS), F32),
            pltpu.VMEM((8, UNIT), F32),
            pltpu.VMEM((8, UNIT), F32),
            pltpu.VMEM((8, UNIT), F32),
            pltpu.VMEM((8, UNIT), F32),
            pltpu.VMEM(back, BF16),
            pltpu.VMEM(back, BF16),
            pltpu.VMEM(back, BF16),
            pltpu.VMEM(back, BF16),
            pltpu.VMEM((2, 4 * UNIT, 4 * UNIT), F32),
            pltpu.VMEM((4, 4 * UNIT, PAIR), BF16),
            pltpu.VMEM((4 * UNIT, 4 * UNIT), BF16),
            pltpu.VMEM((4 * UNIT, 4 * UNIT), BF16),
            pltpu.VMEM((PAIR, 4 * UNIT), F32),
            pltpu.VMEM((2, TILES * TILE, 128), BF16),
            pltpu.VMEM((TILES * TILE, 128), BF16),
            pltpu.VMEM((TILES * TILE, 128), BF16),
            pltpu.VMEM((nplane - 1, depth, 128), BF16),
            pltpu.VMEM((nz, depth, 128), BF16),
            pltpu.VMEM((2, nplane, depth, 128), BF16),
            dma((2, PAIRS)), dma((2, PAIRS)),
            dma((2,)), dma((2,)),
            dma((2, PAIRS)), dma((2, PAIRS)),
            dma, dma,
            dma((nplane - 1,)), dma((nplane - 1,)),
            dma((nz - 1,)), dma((nz - 1,)),
            dma((nplane - 1,)), dma((nplane - 1,)),
            dma, dma,
        ],
        compiler_params=pltpu.CompilerParams(
            collective_id=0, has_side_effects=True, vmem_limit_bytes=48 * 1024 * 1024
        ),
        name="attention_backward",
    )(slide_table, queries, keys, values, outputs, out_grad, out_weight)


def solution(mesh):
    rows = P("rep", "seq", None)
    return jax.shard_map(
        functools.partial(shards, GRID),
        mesh=mesh,
        in_specs=(rows, rows, rows, rows, rows, P(), P("rep", None)),
        out_specs=(rows, rows, rows, P()),
        check_vma=False,
    )
```

time: 313 us -> 54.2 us (0.17); the launches traced: 309 us -> 53.8 us
  waiting for transfers between devices: 148 us -> 0 us
  matrix products: 53.2 us -> 0 us
  starting transfers between devices: 49.4 us -> 0 us
  Pallas kernels: 0 us -> 43.7 us
  local copies, waits for them, and re-layouts: 31.3 us -> 9.46 us
  between operations: 14.8 us -> 0.66 us
  other arithmetic: 11.5 us -> 0 us
    psum x1 -> x0, waiting for transfers between devices: 148 us -> none  [shards(): weight_grad = lax.psum(local_term, ('seq', 'rep')) / math.sqrt(tile_count)]
    dot_general x27 -> x0, matrix products: 53.2 us -> none  [the longest x5 12.4 us: second_visit(): jnp.einsum('hqk,qhd->khd', d_score, q_visit, preferred_element_type=jnp.f...]
    ppermute x12 -> x0, starting transfers between devices: 49.4 us -> none  [from_behind(): lax.ppermute(value, axis, [(source, source + steps) for source in range(f...]
    pallas_call x0 -> x1, Pallas kernels: none -> 43.7 us  [shards(): pl.pallas_call(functools.partial(kernel, grid), out_shape=[jax.ShapeDtype...]
    slice x16 -> x0, local copies, waits for them, and re-layouts: 16.4 us -> none  [the longest x8 8.23 us: second_visit(): d_visit = side_block[1].reshape(row_count, head_count, HEAD)]
    select_n x10 -> x0, other arithmetic: 3.47 us -> none  [the longest x5 3.41 us: second_visit(): totals_in = jnp.where((other_ids >= 0)[None, :], stat_block[0], 1.0)]
    sub x4 -> x0, local copies, waits for them, and re-layouts: 3.39 us -> none  [second_visit(): d_prob - stat_block[1][:, :, None]]
    unnamed x108 -> x18, local copies, waits for them, and re-layouts: 6.82 us -> 9.46 us
  transfers between devices with their start and end apart: 13 -> 0, of which waited for: 1 -> 0; matrix products, arithmetic and copies ran while one was open for 29% -> 0% of each run, Pallas kernels for 0% -> 0%
where the time goes in v1:
time: 54.2 us; the launch traced here: 53.8 us
  Pallas kernels  43.7 us (81%)
  local copies, waits for them, and re-layouts  9.46 us (17%)
  between operations  0.66 us (1%)
    pallas_call x1, Pallas kernels, shards(): pl.pallas_call(functools.partial(kernel, grid), out_shape=[jax.ShapeDtype...  43.7 us
    unnamed x18, local copies, waits for them, and re-layouts  9.46 us

profile of v1, /device:TPU:25, one launch (start us, length us, event | category | flops | bytes accessed | tf_op | source)
XLA Modules:
  0.0 53.8 jit_solution(10351899959856277122)
XLA Ops:
  0.6 0.0 copy-start
  0.6 1.1 %copy-done = bf16[384,768]{1,0:T(8,128)(2,1)S(1)} copy-done((bf16[384,768]{1,0:T(8,128)(2,1)S(1)}, bf16[384,768]{1,0:T(8,128)(2,1)}, u32[]{:S(2)}) %copy-start) | copy-done | bytes 589848
  1.7 0.0 copy-start.1
  1.7 1.0 %copy-done.1 = bf16[1,256,768]{2,1,0:T(8,128)(2,1)S(1)} copy-done((bf16[1,256,768]{2,1,0:T(8,128)(2,1)S(1)}, bf16[1,256,768]{2,1,0:T(8,128)(2,1)}, u32[]{:S(2)}) %copy-start.1) | copy-done | bytes 393240
  2.7 0.0 copy-start.2
  2.7 0.9 %copy-done.2 = bf16[1,256,384]{2,1,0:T(8,128)(2,1)S(1)} copy-done((bf16[1,256,384]{2,1,0:T(8,128)(2,1)S(1)}, bf16[1,256,384]{2,1,0:T(8,128)(2,1)}, u32[]{:S(2)}) %copy-start.2) | copy-done | bytes 196632
  3.6 0.0 copy-start.3
  3.6 0.9 %copy-done.3 = bf16[1,256,384]{2,1,0:T(8,128)(2,1)S(1)} copy-done((bf16[1,256,384]{2,1,0:T(8,128)(2,1)S(1)}, bf16[1,256,384]{2,1,0:T(8,128)(2,1)}, u32[]{:S(2)}) %copy-start.3) | copy-done | bytes 196632
  4.5 0.0 copy-start.4
  4.6 0.9 %copy-done.4 = bf16[1,256,384]{2,1,0:T(8,128)(2,1)S(1)} copy-done((bf16[1,256,384]{2,1,0:T(8,128)(2,1)S(1)}, bf16[1,256,384]{2,1,0:T(8,128)(2,1)}, u32[]{:S(2)}) %copy-start.4) | copy-done | bytes 196632
  5.5 0.0 copy-start.5
  5.5 0.9 %copy-done.5 = bf16[1,256,384]{2,1,0:T(8,128)(2,1)S(1)} copy-done((bf16[1,256,384]{2,1,0:T(8,128)(2,1)S(1)}, bf16[1,256,384]{2,1,0:T(8,128)(2,1)}, u32[]{:S(2)}) %copy-start.5) | copy-done | bytes 196632
  6.4 0.0 copy-start.6
  6.4 0.7 %copy-done.6 = s32[1,128]{1,0:T(1,128)S(1)} copy-done((s32[1,128]{1,0:T(1,128)S(1)}, s32[1,128]{1,0:T(1,128)}, u32[]{:S(2)}) %copy-start.6) | copy-done | bytes 536
  7.1 43.7 %attention_backward.1 = (bf16[1,256,384]{2,1,0:T(8,128)(2,1)S(1)}, bf16[1,256,384]{2,1,0:T(8,128)(2,1)S(1)}, bf16[1,256,384]{2,1,0:T(8,128)(2,1)S(1)}, f32[384,768]{1,0:T(8,128)S(1)}) custom-call(s32[1,128]{1,0:T(1,128)S(1)} %copy-done.6, bf16[1,256,384]{2,1,0:T(8,128)(2,1)S(1)} %copy-done.2, bf16[1,256,384]{2,1,0:T(8,128)(2,1)S(1)} %copy-done.3, ...), custom_call_target="tpu_custom_call" | custom-call | tf_op jit(solution)/shard_map/attention_backward/pallas_call | solution.py:365
  50.7 0.7 %copy.15 = bf16[1,256,384]{2,1,0:T(8,128)(2,1)} copy(bf16[1,256,384]{2,1,0:T(8,128)(2,1)S(1)} %get-tuple-element.8) | data formatting | bytes 393216
  51.4 0.7 %copy.16 = bf16[1,256,384]{2,1,0:T(8,128)(2,1)} copy(bf16[1,256,384]{2,1,0:T(8,128)(2,1)S(1)} %get-tuple-element.9) | data formatting | bytes 393216
  52.1 0.7 %copy.17 = bf16[1,256,384]{2,1,0:T(8,128)(2,1)} copy(bf16[1,256,384]{2,1,0:T(8,128)(2,1)S(1)} %get-tuple-element.10) | data formatting | bytes 393216
  52.8 1.0 %copy.18 = f32[384,768]{1,0:T(8,128)} copy(f32[384,768]{1,0:T(8,128)S(1)} %get-tuple-element.11) | data formatting | bytes 2359296
Async XLA Ops:
  0.6 1.1 %copy-start = (bf16[384,768]{1,0:T(8,128)(2,1)S(1)}, bf16[384,768]{1,0:T(8,128)(2,1)}, u32[]{:S(2)}) copy-start(bf16[384,768]{1,0:T(8,128)(2,1)} %w.1) | copy-start | bytes 1769476
  1.7 1.0 %copy-start.1 = (bf16[1,256,768]{2,1,0:T(8,128)(2,1)S(1)}, bf16[1,256,768]{2,1,0:T(8,128)(2,1)}, u32[]{:S(2)}) copy-start(bf16[1,256,768]{2,1,0:T(8,128)(2,1)} %dy.1) | copy-start | bytes 1179652
  2.7 0.9 %copy-start.2 = (bf16[1,256,384]{2,1,0:T(8,128)(2,1)S(1)}, bf16[1,256,384]{2,1,0:T(8,128)(2,1)}, u32[]{:S(2)}) copy-start(bf16[1,256,384]{2,1,0:T(8,128)(2,1)} %q.1) | copy-start | bytes 589828
  3.6 0.9 %copy-start.3 = (bf16[1,256,384]{2,1,0:T(8,128)(2,1)S(1)}, bf16[1,256,384]{2,1,0:T(8,128)(2,1)}, u32[]{:S(2)}) copy-start(bf16[1,256,384]{2,1,0:T(8,128)(2,1)} %k.1) | copy-start | bytes 589828
  4.5 0.9 %copy-start.4 = (bf16[1,256,384]{2,1,0:T(8,128)(2,1)S(1)}, bf16[1,256,384]{2,1,0:T(8,128)(2,1)}, u32[]{:S(2)}) copy-start(bf16[1,256,384]{2,1,0:T(8,128)(2,1)} %v.1) | copy-start | bytes 589828
  5.5 0.9 %copy-start.5 = (bf16[1,256,384]{2,1,0:T(8,128)(2,1)S(1)}, bf16[1,256,384]{2,1,0:T(8,128)(2,1)}, u32[]{:S(2)}) copy-start(bf16[1,256,384]{2,1,0:T(8,128)(2,1)} %o.1) | copy-start | bytes 589828
  6.4 0.7 %copy-start.6 = (s32[1,128]{1,0:T(1,128)S(1)}, s32[1,128]{1,0:T(1,128)}, u32[]{:S(2)}) copy-start(s32[1,128]{1,0:T(1,128)} %tab.1) | copy-start | bytes 1540

commit v2 on v1

--- a/solution.py
+++ b/solution.py
@@ -46,11 +46,12 @@
 
 
 def kernel(
-    grid, tab, q, k, v, o, dy, w,
-    dq, dk, dv, wg,
+    grid, tab, q_in, k_in, v_in, o_in, dy_in, w_in,
+    dq_out, dk_out, dv_out, final_out,
+    q, k, v, o, dy, w, load_sem, dq, dk, dv, final, out_sem,
     d_own, snd_l, snd_r, rcv_l, rcv_r, del_own, del_sl, del_sr, del_rl, del_rr,
     ret_sl, ret_sr, ret_rl, ret_rr, bias, win, p_buf, s_buf, q_turn,
-    term, core_in, plane_out, plane_in, line, final,
+    term, core_in, plane_out, plane_in, line,
     halo_send, halo_recv, del_send, del_recv, ret_send, ret_recv,
     core_send, core_recv, plane_send, plane_recv, line_send, line_recv,
     share_send, share_recv, swap_send, swap_recv,
@@ -91,6 +92,15 @@
     for offset in range(1, nz):
         pl.semaphore_signal(barrier, inc=1, device_id=line_peer(offset), device_id_type=MESH)
 
+    loads = [
+        pltpu.make_async_copy(src, dst, load_sem.at[i])
+        for i, (src, dst) in enumerate(
+            ((dy_in, dy), (w_in, w), (o_in, o), (q_in, q), (k_in, k), (v_in, v))
+        )
+    ]
+    for c in loads:
+        c.start()
+
     first = 2 * seq
     last_unit = 2 * nseq - 1
 
@@ -127,6 +137,8 @@
             device_id=peer, device_id_type=MESH,
         )
 
+    for c in loads[:3]:
+        c.wait()
     d_own[...] = nt(dy[0], w[...]).astype(BF16)
     prod = d_own[...].astype(F32) * o[0].astype(F32)
     upper = prod.astype(BF16)
@@ -151,6 +163,8 @@
     del_sl[6:8] = jnp.zeros((2, UNIT), F32)
     del_sr[6:8] = jnp.zeros((2, UNIT), F32)
 
+    for c in loads[3:]:
+        c.wait()
     sources = (q, k, v, None)
     for p in range(PAIRS):
         cols = slice(p * PAIR, (p + 1) * PAIR)
@@ -183,14 +197,25 @@
         go(copy(del_sl, del_rr, del_send.at[0], del_recv.at[0], to_left)),
         go(copy(del_sr, del_rl, del_send.at[1], del_recv.at[1], to_right)),
     ]
-    halo_in = []
-    for p in range(PAIRS):
-        halo_in.append([
-            go(copy(snd_l.at[p], rcv_r.at[p], halo_send.at[0, p], halo_recv.at[0, p], to_left)),
-            go(copy(snd_r.at[p], rcv_l.at[p], halo_send.at[1, p], halo_recv.at[1, p], to_right)),
-        ])
-        if p == 0:
-            core_copy = go(copy(term.at[1 - core], core_in, core_send, core_recv, to_core))
+    halo_l = [
+        copy(snd_l.at[p], rcv_r.at[p], halo_send.at[0, p], halo_recv.at[0, p], to_left)
+        for p in range(PAIRS)
+    ]
+    halo_r = [
+        copy(snd_r.at[p], rcv_l.at[p], halo_send.at[1, p], halo_recv.at[1, p], to_right)
+        for p in range(PAIRS)
+    ]
+    edge_l, edge_r = z == 0, z == nz - 1
+
+    def forward(p, edges):
+        for c, edge in ((halo_l[p], edge_l), (halo_r[p], edge_r)):
+            if edges is None:
+                c.start()
+            else:
+                pl.when(edge if edges else jnp.logical_not(edge))(c.start)
+
+    core_copy = go(copy(term.at[1 - core], core_in, core_send, core_recv, to_core))
+    forward(0, None)
 
     for par in range(2):
         mine_away = split_l if par else split_r
@@ -222,11 +247,15 @@
             plane_send.at[offset - 1], plane_recv.at[offset - 1], peer,
         )))
 
+    forward(1, False)
+
     scale = 0.125 * math.log2(math.e)
 
+    def arrive(p):
+        halo_l[p].wait_recv()
+        halo_r[p].wait_recv()
+
     def attend(p):
-        for c in halo_in[p]:
-            c.wait_recv()
         cols = slice(p * PAIR, (p + 1) * PAIR)
         for i, src in enumerate(sources):
             win[i, :UNIT] = low_from(split_l, rcv_l[p, i], rcv_r[p, i])
@@ -279,14 +308,22 @@
             before, after = grad[:UNIT], grad[3 * UNIT:]
             ret_sl[p, i] = low_from(split_r, before, after)
             ret_sr[p, i] = high_from(split_l, after, before)
-        return [
+
+    returns = []
+
+    def give_back(p):
+        returns.append([
             go(copy(ret_sl.at[p], ret_rr.at[p], ret_send.at[0, p], ret_recv.at[0, p], to_left)),
             go(copy(ret_sr.at[p], ret_rl.at[p], ret_send.at[1, p], ret_recv.at[1, p], to_right)),
-        ]
+        ])
 
     for c in deltas_in:
         c.wait_recv()
-    returns = [attend(0)]
+    arrive(0)
+    forward(2, False)
+    forward(1, True)
+    attend(0)
+    forward(2, True)
 
     for c in plane_copies:
         c.wait_recv()
@@ -301,7 +338,10 @@
             line_peer(offset),
         )))
 
-    returns.append(attend(1))
+    give_back(0)
+    arrive(1)
+    attend(1)
+    give_back(1)
 
     for c in line_copies:
         c.wait_recv()
@@ -318,11 +358,9 @@
             share_send.at[offset - 1], share_recv.at[offset - 1], peer,
         )))
 
-    returns.append(attend(2))
-
-    for c in share_copies:
-        c.wait_recv()
-    swap = go(copy(final.at[core], final.at[core], swap_send, swap_recv, to_core))
+    arrive(2)
+    attend(2)
+    give_back(2)
 
     for p in range(PAIRS):
         for c in returns[p]:
@@ -338,8 +376,42 @@
                 2 * HEAD - HEAD * (2 * sent_r + split_l), ub, from_r
             )
 
+    writes = [
+        pltpu.make_async_copy(src, dst, out_sem.at[i])
+        for i, (src, dst) in enumerate(((dq, dq_out), (dk, dk_out), (dv, dv_out)))
+    ]
+    for c in writes:
+        c.start()
+
+    for c in share_copies:
+        c.wait_recv()
+    swap = go(copy(final.at[core], final.at[core], swap_send, swap_recv, to_core))
+
+    writes.append(pltpu.make_async_copy(final.at[core], final_out.at[core], out_sem.at[3]))
+    writes[-1].start()
     swap.wait_recv()
+    writes.append(
+        pltpu.make_async_copy(final.at[1 - core], final_out.at[1 - core], out_sem.at[4])
+    )
+    writes[-1].start()
+    for c in sends + halo_l + halo_r:
+        c.wait_send()
+    for c in writes:
+        c.wait()
+
+
+def finish(nplane, dq, dk, dv, total, dq_out, dk_out, dv_out, wg_out, parts, final, wg, sem):
+    flows = ((dq, dq_out), (dk, dk_out), (dv, dv_out))
+    loads = [
+        pltpu.make_async_copy(total.at[h], final.at[h], sem.at[h]) for h in range(2)
+    ] + [
+        pltpu.make_async_copy(src, parts.at[i], sem.at[2 + i]) for i, (src, _) in enumerate(flows)
+    ]
+    for c in loads:
+        c.start()
+    copies = []
     for h in range(2):
+        loads[h].wait()
         for index in range(nplane):
             begin = (index * TILES) // nplane
             end = ((index + 1) * TILES) // nplane
@@ -348,9 +420,15 @@
                 wg[h * HALF + row:h * HALF + row + TILE, j * 128:(j + 1) * 128] = final[
                     h, index, (t - begin) * TILE:(t - begin + 1) * TILE
                 ].astype(F32)
-
-    for c in sends:
-        c.wait_send()
+        rows = pl.ds(h * HALF, HALF)
+        copies.append(pltpu.make_async_copy(wg.at[rows], wg_out.at[rows], sem.at[5 + h]))
+        copies[-1].start()
+    for i, (_, dst) in enumerate(flows):
+        loads[2 + i].wait()
+        copies.append(pltpu.make_async_copy(parts.at[i], dst, sem.at[7 + i]))
+        copies[-1].start()
+    for c in copies:
+        c.wait()
 
 
 def shards(grid, queries, keys, values, outputs, out_grad, out_weight, slide_table):
@@ -358,17 +436,23 @@
     nplane = nx * nyl * nyh
     depth = -(-TILES // nplane) * TILE
     dma = pltpu.SemaphoreType.DMA
-    vmem = pl.BlockSpec(memory_space=pltpu.VMEM)
     part = (1, ROWS, FEATS)
     halo = (PAIRS, 4, UNIT, PAIR)
     back = (PAIRS, 3, UNIT, PAIR)
-    return pl.pallas_call(
+    parts = pl.pallas_call(
         functools.partial(kernel, grid),
         out_shape=[jax.ShapeDtypeStruct(part, BF16)] * 3
-        + [jax.ShapeDtypeStruct((FEATS, WIDTH), F32)],
-        in_specs=[pl.BlockSpec(memory_space=pltpu.SMEM)] + [vmem] * 6,
-        out_specs=[vmem] * 4,
+        + [jax.ShapeDtypeStruct((2, nplane, depth, 128), BF16)],
+        in_specs=[pl.BlockSpec(memory_space=pltpu.SMEM)] + [pl.BlockSpec(memory_space=pl.ANY)] * 6,
+        out_specs=[pl.BlockSpec(memory_space=pl.ANY)] * 4,
         scratch_shapes=[
+            *[pltpu.VMEM(part, BF16)] * 4,
+            pltpu.VMEM((1, ROWS, WIDTH), BF16),
+            pltpu.VMEM((FEATS, WIDTH), BF16),
+            dma((6,)),
+            *[pltpu.VMEM(part, BF16)] * 3,
+            pltpu.VMEM((2, nplane, depth, 128), BF16),
+            dma((5,)),
             pltpu.VMEM((ROWS, FEATS), BF16),
             pltpu.VMEM(halo, BF16),
             pltpu.VMEM(halo, BF16),
@@ -393,7 +477,6 @@
             pltpu.VMEM((TILES * TILE, 128), BF16),
             pltpu.VMEM((nplane - 1, depth, 128), BF16),
             pltpu.VMEM((nz, depth, 128), BF16),
-            pltpu.VMEM((2, nplane, depth, 128), BF16),
             dma((2, PAIRS)), dma((2, PAIRS)),
             dma((2,)), dma((2,)),
             dma((2, PAIRS)), dma((2, PAIRS)),
@@ -404,10 +487,25 @@
             dma, dma,
         ],
         compiler_params=pltpu.CompilerParams(
-            collective_id=0, has_side_effects=True, vmem_limit_bytes=48 * 1024 * 1024
+            collective_id=0, has_side_effects=True, vmem_limit_bytes=56 * 1024 * 1024
         ),
         name="attention_backward",
     )(slide_table, queries, keys, values, outputs, out_grad, out_weight)
+    return pl.pallas_call(
+        functools.partial(finish, nplane),
+        out_shape=[jax.ShapeDtypeStruct(part, BF16)] * 3
+        + [jax.ShapeDtypeStruct((FEATS, WIDTH), F32)],
+        in_specs=[pl.BlockSpec(memory_space=pl.ANY)] * 4,
+        out_specs=[pl.BlockSpec(memory_space=pl.ANY)] * 4,
+        scratch_shapes=[
+            pltpu.VMEM((3, *part), BF16),
+            pltpu.VMEM((2, nplane, depth, 128), BF16),
+            pltpu.VMEM((FEATS, WIDTH), F32),
+            dma((10,)),
+        ],
+        compiler_params=pltpu.CompilerParams(vmem_limit_bytes=56 * 1024 * 1024),
+        name="results",
+    )(*parts)
 
 
 def solution(mesh):

time: 54.2 us -> 46.7 us (0.86)
  the two profiles are of different devices: /device:TPU:25 before, /device:TPU:1 now
where the time goes in v2:
time: 46.7 us; the launch traced here: 46.6 us
  Pallas kernels  46 us (99%)
  between operations  0.64 us (1%)
    pallas_call x1, Pallas kernels, shards(): pl.pallas_call(functools.partial(kernel, grid), out_shape=[jax.ShapeDtype...  43.7 us
    pallas_call x1, Pallas kernels, shards(): pl.pallas_call(functools.partial(finish, nplane), out_shape=[jax.ShapeDty...  2.29 us

profile of v2, /device:TPU:1, one launch (start us, length us, event | category | flops | bytes accessed | tf_op | source)
XLA Modules:
  0.0 46.6 jit_solution(4944658196759977921)
XLA Ops:
  0.6 43.7 %attention_backward.1 = (bf16[1,256,384]{2,1,0:T(8,128)(2,1)}, bf16[1,256,384]{2,1,0:T(8,128)(2,1)}, bf16[1,256,384]{2,1,0:T(8,128)(2,1)}, bf16[2,16,80,128]{3,2,1,0:T(8,128)(2,1)}) custom-call(s32[1,128]{1,0:T(1,128)} %tab.1, bf16[1,256,384]{2,1,0:T(8,128)(2,1)} %q_in.1, bf16[1,256,384]{2,1,0:T(8,128)(2,1)} %k_in.1, bf16[1,256,384]{2,1,0:T(8,128)(2,1)} %v_in.1, ...), custom_call_target="tpu_custom_call" | custom-call | tf_op jit(solution)/shard_map/attention_backward/pallas_call | solution.py:442
  44.3 2.3 %results.1 = (bf16[1,256,384]{2,1,0:T(8,128)(2,1)}, bf16[1,256,384]{2,1,0:T(8,128)(2,1)}, bf16[1,256,384]{2,1,0:T(8,128)(2,1)}, f32[384,768]{1,0:T(8,128)}) custom-call(bf16[1,256,384]{2,1,0:T(8,128)(2,1)} %get-tuple-element.8.dq, bf16[1,256,384]{2,1,0:T(8,128)(2,1)} %get-tuple-element.9.dk, bf16[1,256,384]{2,1,0:T(8,128)(2,1)} %get-tuple-element.10.dv, ...), custom_call_target="tpu_custom_call" | custom-call | tf_op jit(solution)/shard_map/results/pallas_call | solution.py:494

commit v3 on v2

--- a/solution.py
+++ b/solution.py
@@ -186,6 +186,34 @@
 
     pl.semaphore_wait(barrier, 3 + (nplane - 1) + (nz - 1))
 
+    short = TILES // nplane * TILE
+
+    def has_tail(index):
+        return ((index + 1) * TILES) // nplane - (index * TILES) // nplane > TILES // nplane
+
+    class Chunk:
+        def __init__(self, index, make):
+            self.either = ((make(short), jnp.logical_not(has_tail(index))),
+                           (make(depth), has_tail(index)))
+            if short == depth:
+                self.either = ((make(depth), None),)
+
+        def each(self, name):
+            for c, cond in self.either:
+                if cond is None:
+                    getattr(c, name)()
+                else:
+                    pl.when(cond)(getattr(c, name))
+
+        def start(self):
+            self.each("start")
+
+        def wait_recv(self):
+            self.each("wait_recv")
+
+        def wait_send(self):
+            self.each("wait_send")
+
     sends = []
 
     def go(c):
@@ -236,16 +264,21 @@
     core_copy.wait_recv()
     plane_out[...] = (term[core].astype(F32) + core_in[...].astype(F32)).astype(BF16)
 
-    def chunk(index):
-        return pl.ds(pl.multiple_of((index * TILES) // nplane * TILE, TILE), depth)
-
-    plane_copies = []
+    def chunk(index, rows):
+        return pl.ds(pl.multiple_of((index * TILES) // nplane * TILE, TILE), rows)
+
+    plane_in_copies = []
     for offset in range(1, nplane):
         other, peer = plane_peer(offset)
-        plane_copies.append(go(copy(
-            plane_out.at[chunk(other)], plane_in.at[offset - 1],
-            plane_send.at[offset - 1], plane_recv.at[offset - 1], peer,
-        )))
+
+        def make(rows, other=other, peer=peer, i=offset - 1):
+            return copy(
+                plane_out.at[chunk(other, rows)], plane_in.at[i, pl.ds(0, rows)],
+                plane_send.at[i], plane_recv.at[i], peer,
+            )
+
+        go(Chunk(other, make))
+        plane_in_copies.append(Chunk(spot, make))
 
     forward(1, False)
 
@@ -322,21 +355,21 @@
     arrive(0)
     forward(2, False)
     forward(1, True)
+    forward(2, True)
     attend(0)
-    forward(2, True)
-
-    for c in plane_copies:
+
+    for c in plane_in_copies:
         c.wait_recv()
-    total = plane_out[chunk(spot)].astype(F32)
+    total = plane_out[chunk(spot, depth)].astype(F32)
     for offset in range(1, nplane):
         total = total + plane_in[offset - 1].astype(F32)
     line[z] = total.astype(BF16)
     line_copies = []
     for offset in range(1, nz):
-        line_copies.append(go(copy(
-            line.at[z], line.at[z], line_send.at[offset - 1], line_recv.at[offset - 1],
-            line_peer(offset),
-        )))
+        line_copies.append(go(Chunk(spot, lambda rows, offset=offset: copy(
+            line.at[z, pl.ds(0, rows)], line.at[z, pl.ds(0, rows)],
+            line_send.at[offset - 1], line_recv.at[offset - 1], line_peer(offset),
+        ))))
 
     give_back(0)
     arrive(1)
@@ -350,13 +383,22 @@
         total = total + line[index].astype(F32)
     norm = 1.0 / math.sqrt(nseq * ROWS * nyh * ncore)
     final[core, spot] = (total * norm).astype(BF16)
-    share_copies = []
+
+    def passed(index, i):
+        def make(rows):
+            part = final.at[core, index, pl.ds(0, rows)]
+            return copy(part, part, swap_send.at[i], swap_recv.at[i], to_core)
+        return Chunk(index, make)
+
+    def shared(index, i, peer):
+        def make(rows):
+            part = final.at[core, index, pl.ds(0, rows)]
+            return copy(part, part, share_send.at[i], share_recv.at[i], peer)
+        return Chunk(index, make)
+
     for offset in range(1, nplane):
-        _, peer = plane_peer(offset)
-        share_copies.append(go(copy(
-            final.at[core, spot], final.at[core, spot],
-            share_send.at[offset - 1], share_recv.at[offset - 1], peer,
-        )))
+        go(shared(spot, offset - 1, plane_peer(offset)[1]))
+    go(passed(spot, 0))
 
     arrive(2)
     attend(2)
@@ -383,13 +425,14 @@
     for c in writes:
         c.start()
 
-    for c in share_copies:
-        c.wait_recv()
-    swap = go(copy(final.at[core], final.at[core], swap_send, swap_recv, to_core))
-
+    for offset in range(1, nplane):
+        source = lax.rem(spot + nplane - offset, nplane)
+        shared(source, offset - 1, to_core).wait_recv()
+        go(passed(source, offset))
     writes.append(pltpu.make_async_copy(final.at[core], final_out.at[core], out_sem.at[3]))
     writes[-1].start()
-    swap.wait_recv()
+    for offset in range(nplane):
+        passed(lax.rem(spot + nplane - offset, nplane), offset).wait_recv()
     writes.append(
         pltpu.make_async_copy(final.at[1 - core], final_out.at[1 - core], out_sem.at[4])
     )
@@ -484,7 +527,7 @@
             dma((nplane - 1,)), dma((nplane - 1,)),
             dma((nz - 1,)), dma((nz - 1,)),
             dma((nplane - 1,)), dma((nplane - 1,)),
-            dma, dma,
+            dma((nplane,)), dma((nplane,)),
         ],
         compiler_params=pltpu.CompilerParams(
             collective_id=0, has_side_effects=True, vmem_limit_bytes=56 * 1024 * 1024

time: 46.7 us -> 46 us (0.985)
  the two profiles are of different devices: /device:TPU:1 before, /device:TPU:25 now
where the time goes in v3:
time: 46 us; the launch traced here: 45.9 us
  Pallas kernels  45.3 us (98%)
  between operations  0.64 us (1%)
    pallas_call x1, Pallas kernels, shards(): pl.pallas_call(functools.partial(kernel, grid), out_shape=[jax.ShapeDtype...  43 us
    pallas_call x1, Pallas kernels, shards(): pl.pallas_call(functools.partial(finish, nplane), out_shape=[jax.ShapeDty...  2.29 us

profile of v3, /device:TPU:25, one launch (start us, length us, event | category | flops | bytes accessed | tf_op | source)
XLA Modules:
  0.0 45.9 jit_solution(5491497039343496885)
XLA Ops:
  0.6 43.0 %attention_backward.1 = (bf16[1,256,384]{2,1,0:T(8,128)(2,1)}, bf16[1,256,384]{2,1,0:T(8,128)(2,1)}, bf16[1,256,384]{2,1,0:T(8,128)(2,1)}, bf16[2,16,80,128]{3,2,1,0:T(8,128)(2,1)}) custom-call(s32[1,128]{1,0:T(1,128)} %tab.1, bf16[1,256,384]{2,1,0:T(8,128)(2,1)} %q_in.1, bf16[1,256,384]{2,1,0:T(8,128)(2,1)} %k_in.1, bf16[1,256,384]{2,1,0:T(8,128)(2,1)} %v_in.1, ...), custom_call_target="tpu_custom_call" | custom-call | tf_op jit(solution)/shard_map/attention_backward/pallas_call | solution.py:485
  43.6 2.3 %results.1 = (bf16[1,256,384]{2,1,0:T(8,128)(2,1)}, bf16[1,256,384]{2,1,0:T(8,128)(2,1)}, bf16[1,256,384]{2,1,0:T(8,128)(2,1)}, f32[384,768]{1,0:T(8,128)}) custom-call(bf16[1,256,384]{2,1,0:T(8,128)(2,1)} %get-tuple-element.8.dq, bf16[1,256,384]{2,1,0:T(8,128)(2,1)} %get-tuple-element.9.dk, bf16[1,256,384]{2,1,0:T(8,128)(2,1)} %get-tuple-element.10.dv, ...), custom_call_target="tpu_custom_call" | custom-call | tf_op jit(solution)/shard_map/results/pallas_call | solution.py:537

commit v4 on v3

--- a/solution.py
+++ b/solution.py
@@ -281,6 +281,7 @@
         plane_in_copies.append(Chunk(spot, make))
 
     forward(1, False)
+    forward(2, False)
 
     scale = 0.125 * math.log2(math.e)
 
@@ -353,7 +354,6 @@
     for c in deltas_in:
         c.wait_recv()
     arrive(0)
-    forward(2, False)
     forward(1, True)
     forward(2, True)
     attend(0)

time: 46 us -> 46 us (level)
  no operation moved by 1% of the time
where the time goes in v4:
time: 46 us; the launch traced here: 45.9 us
  Pallas kernels  45.2 us (98%)
  between operations  0.64 us (1%)
    pallas_call x1, Pallas kernels, shards(): pl.pallas_call(functools.partial(kernel, grid), out_shape=[jax.ShapeDtype...  43 us
    pallas_call x1, Pallas kernels, shards(): pl.pallas_call(functools.partial(finish, nplane), out_shape=[jax.ShapeDty...  2.29 us

profile of v4, /device:TPU:25, one launch (start us, length us, event | category | flops | bytes accessed | tf_op | source)
XLA Modules:
  0.0 45.9 jit_solution(12280942300686112105)
XLA Ops:
  0.6 43.0 %attention_backward.1 = (bf16[1,256,384]{2,1,0:T(8,128)(2,1)}, bf16[1,256,384]{2,1,0:T(8,128)(2,1)}, bf16[1,256,384]{2,1,0:T(8,128)(2,1)}, bf16[2,16,80,128]{3,2,1,0:T(8,128)(2,1)}) custom-call(s32[1,128]{1,0:T(1,128)} %tab.1, bf16[1,256,384]{2,1,0:T(8,128)(2,1)} %q_in.1, bf16[1,256,384]{2,1,0:T(8,128)(2,1)} %k_in.1, bf16[1,256,384]{2,1,0:T(8,128)(2,1)} %v_in.1, ...), custom_call_target="tpu_custom_call" | custom-call | tf_op jit(solution)/shard_map/attention_backward/pallas_call | solution.py:485
  43.6 2.3 %results.1 = (bf16[1,256,384]{2,1,0:T(8,128)(2,1)}, bf16[1,256,384]{2,1,0:T(8,128)(2,1)}, bf16[1,256,384]{2,1,0:T(8,128)(2,1)}, f32[384,768]{1,0:T(8,128)}) custom-call(bf16[1,256,384]{2,1,0:T(8,128)(2,1)} %get-tuple-element.8.dq, bf16[1,256,384]{2,1,0:T(8,128)(2,1)} %get-tuple-element.9.dk, bf16[1,256,384]{2,1,0:T(8,128)(2,1)} %get-tuple-element.10.dv, ...), custom_call_target="tpu_custom_call" | custom-call | tf_op jit(solution)/shard_map/results/pallas_call | solution.py:537
